TPU v7x, 32 devices: a whole 2x2x4 slice. The times are simulated.
32 devices in a mesh: gx: 8 (over y, x, core), gy: 4 (over z).
Axes of the slice: x: 2, y: 2, z: 4, core: 2. Of those that a mesh axis runs over, the one named last changes fastest.
Arguments:
- sources: bfloat16 [8, 4, 8, 64, 256], P('gx', 'gy'), may hold values from -12 to 12
- geometry: bfloat16 [8, 4, 8, 4, 256], P('gx', 'gy'), may hold values from -0.5 to 0.5, as said below
- near_lists: int32 [8, 4, 8, 24], P('gx', 'gy'), may hold values from -1 to 255, as said below
- far_lists: int32 [8, 4, 4, 16], P('gx', 'gy'), may hold values from 0 to 7, as said below
- bases_in: bfloat16 [8, 4, 4, 32, 8, 256], P('gx', 'gy')
- bases_out: bfloat16 [8, 4, 4, 32, 8, 256], P('gx', 'gy'), may hold values from -0.25 to 0.25
- couplings: float32 [8, 4, 4, 32, 512], P('gx', 'gy')
Outputs:
- potential: float32 [8, 4, 8, 64, 256], P('gx', 'gy')
Inputs may be any that keep to these rules, and one draw needn't show every extreme that they name: `near_lists`: for each leaf the first c entries are live, c between 1 and 24 and equal to 24 on some leaves and to 1 on others; the first is the leaf itself, and every live entry names a leaf on a device whose gx and gy indices differ from the leaf's by at most one, in a slot that differs from the leaf's slot by at most one; the other entries are -1. `far_lists`: level 0 entries are below 4, levels 1 and 2 below 8, level 3 below 2. `geometry`: rows 0 to 2 lie in [-0.5, 0.5], row 3 about 0.006 to 0.04.
All inputs are finite; a program needn't handle non-finite values.
Results may differ from a plain program's by a relative error of at most 0.0029.
Values may be sent and summed in bfloat16 or wider, within the bound.
A program may use at most 64 MiB of HBM per device.

v0:
```python
import math
import jax
import jax.numpy as jnp
from jax import lax
from jax.sharding import PartitionSpec as P

FOUR_PI = 4.0 * math.pi


def from_partner(x, axis, stride):
    return lax.ppermute(x, axis, [(i, i ^ 1 << stride) for i in range(lax.axis_size(axis))])


def extended(block, sides, width):
    for axis, dim in sides:
        count = lax.axis_size(axis)
        forward = [(i, i + 1) for i in range(count - 1)]
        backward = [(target, source) for source, target in forward]
        low = lax.ppermute(
            lax.slice_in_dim(block, block.shape[dim] - width, None, axis=dim), axis, forward
        )
        high = lax.ppermute(lax.slice_in_dim(block, 0, width, axis=dim), axis, backward)
        block = jnp.concatenate([low, block, high], axis=dim)
    return block


def near_block(target_geo, target_center, source_geo, source_center, source_vals, weight):
    target_pos = target_geo[:, :3, :].astype(jnp.float32) + target_center[:, :, None]
    source_pos = source_geo[:, :3, :].astype(jnp.float32) + source_center[:, :, None]
    squared = jnp.zeros(
        (target_pos.shape[0], target_pos.shape[2], source_pos.shape[2]), jnp.float32
    )
    for component in range(3):
        offset = target_pos[:, component, :, None] - source_pos[:, component, None, :]
        squared = squared + offset * offset
    panel_area = source_geo[:, 3, :].astype(jnp.float32)[:, None, :]
    kernel = (
        weight[:, None, None] * panel_area / (FOUR_PI * jnp.sqrt(squared + panel_area))
    ).astype(jnp.bfloat16)
    return jnp.einsum("lij,lrj->lri", kernel, source_vals, preferred_element_type=jnp.float32)


def column_level_sums(first_term, second_term, third_term):
    first_sum = first_term
    for bit in range(2):
        first_sum = first_sum + from_partner(first_sum, "gy", bit)
    second_sum, third_sum = lax.psum((second_term, third_term), "gy")
    return (first_sum, second_sum, third_sum)


def coarse_total(values):
    for bit in range(2):
        values = values + from_partner(values, "gx", bit)
    return values


def body(sources, geometry, near_lists, far_lists, bases_in, bases_out, couplings):
    leaf_dev = sources.shape[2]
    rhs_cols = sources.shape[3]
    panels = sources.shape[4]
    slot_total = near_lists.shape[3]
    row_pos = lax.axis_index("gx")
    col_pos = lax.axis_index("gy")
    col_devs = lax.axis_size("gy")
    packed = jnp.concatenate([sources, geometry], axis=3)
    block = extended(packed, (("gx", 0), ("gy", 1)), 1)
    block = block.reshape((9 * leaf_dev,) + packed.shape[3:])
    lists = near_lists[0, 0]
    live = lists >= 0
    safe = jnp.maximum(lists, 0)
    device = safe // leaf_dev
    src_row = device // col_devs
    src_col = device % col_devs
    src_leaf = safe % leaf_dev
    local = ((src_row - row_pos + 1) * 3 + (src_col - col_pos + 1)) * leaf_dev + src_leaf
    local = jnp.where(live, local, 4 * leaf_dev)
    centers = jnp.stack([src_row, src_col, src_leaf], axis=-1).astype(jnp.float32)
    weights = live.astype(jnp.float32)
    own_leaf = jnp.arange(leaf_dev, dtype=jnp.int32)
    own_center = jnp.stack(
        [jnp.zeros_like(own_leaf) + row_pos, jnp.zeros_like(own_leaf) + col_pos, own_leaf], axis=-1
    ).astype(jnp.float32)
    target_geo = geometry[0, 0]
    start_total = jnp.zeros((leaf_dev, rhs_cols, panels), jnp.float32)

    def add_slot(slot, total):
        index = lax.dynamic_index_in_dim(local, slot, 1, keepdims=False)
        chosen = jnp.take(block, index, axis=0)
        center = lax.dynamic_index_in_dim(centers, slot, 1, keepdims=False)
        weight = lax.dynamic_index_in_dim(weights, slot, 1, keepdims=False)
        return total + near_block(
            target_geo, own_center, chosen[:, rhs_cols:], center, chosen[:, :rhs_cols], weight
        )

    near_field = lax.fori_loop(0, slot_total, add_slot, start_total)
    projection = jnp.einsum(
        "aqlp,lrp->aqr", bases_in[0, 0], sources[0, 0], preferred_element_type=jnp.float32
    )
    first_sum, second_sum, column_three = column_level_sums(
        projection[1], projection[2], projection[3]
    )
    column_table = lax.all_gather(projection[0][None], "gy", axis=0, tiled=True)
    third_sum = coarse_total(column_three)
    table_one, table_two, table_three = (
        lax.all_gather(first_sum[None], "gx", axis=0, tiled=True),
        lax.all_gather(second_sum[None], "gx", axis=0, tiled=True),
        lax.all_gather(third_sum[None], "gx", axis=0, tiled=True),
    )
    table_three = table_three[::4]
    tables = (column_table, table_one, table_two, table_three)
    far_ids = far_lists[0, 0]
    gathered = jnp.stack([jnp.take(tables[level], far_ids[level], axis=0) for level in range(4)])
    gathered = gathered.reshape(4, -1, rhs_cols)
    interaction = jnp.einsum(
        "aqk,akr->aqr", couplings[0, 0], gathered, precision=lax.Precision.HIGHEST
    )
    summed_one, summed_two, summed_column = column_level_sums(
        interaction[1], interaction[2], interaction[3]
    )
    summed_three = coarse_total(summed_column)
    target_sum = jnp.stack([interaction[0], summed_one, summed_two, summed_three]).astype(
        jnp.bfloat16
    )
    far_field = jnp.einsum(
        "aqr,aqlp->lrp", target_sum, bases_out[0, 0], preferred_element_type=jnp.float32
    )
    return (near_field + far_field).reshape(sources.shape)


def solution(mesh):
    in_specs = (
        P("gx", "gy", None, None, None),
        P("gx", "gy", None, None, None),
        P("gx", "gy", None, None),
        P("gx", "gy", None, None),
        P("gx", "gy", None, None, None, None),
        P("gx", "gy", None, None, None, None),
        P("gx", "gy", None, None, None),
    )
    out_specs = P("gx", "gy", None, None, None)
    return jax.shard_map(body, mesh=mesh, in_specs=in_specs, out_specs=out_specs, check_vma=False)
```

profile of v0, /device:TPU:0, one launch (start us, length us, event | category | flops | bytes accessed | tf_op | source)
XLA Modules:
  0.0 249.7 jit_solution(3222020537244776442)
XLA Ops:
  1.9 2.4 collective-permute-start
  7.0 20.1 %all-reduce.1 = (f32[32,64]{1,0:T(8,128)S(1)}, f32[1,32,64]{2,1,0:T(8,128)S(1)}) all-reduce(f32[32,64]{1,0:T(8,128)S(1)} %get-tuple-element.230, f32[1,32,64]{2,1,0:T(8,128)S(1)} %get-tuple-element.231), channel_id=1, replica_groups=mesh['gx'=8,'gy'=4] {'gy'}, use_global_device_ids=true, to_apply=%region_3.5 | all-reduce | flops 4096 | bytes 32768 | tf_op jit(solution)/shard_map/psum | solution.py:47
  30.3 13.1 %all_gather.12 = f32[4,32,64]{2,1,0:T(8,128)S(1)} all-gather(f32[1,32,64]{2,1,0:T(8,128)S(1)} %get-tuple-element.229), channel_id=1, replica_groups=mesh['gx'=8,'gy'=4] {'gy'}, dimensions={0}, use_global_device_ids=true | all-gather | bytes 40960 | tf_op jit(solution)/shard_map/all_gather | solution.py:102
  44.6 12.6 %all_gather.14 = f32[8,32,64]{2,1,0:T(8,128)S(1)} all-gather(f32[1,32,64]{2,1,0:T(8,128)S(1)} %get-tuple-element.208), channel_id=1, replica_groups=mesh['gx'=8,'gy'=4] {'gx'}, dimensions={0}, use_global_device_ids=true | all-gather | bytes 73728 | tf_op jit(solution)/shard_map/all_gather | solution.py:106
  59.2 2.5 collective-permute-done.7
  61.7 8.4 %all-gather.1 = f32[256,64]{1,0:T(8,128)S(1)} all-gather(f32[32,64]{1,0:T(8,128)S(1)} %add.271), channel_id=3, replica_groups=mesh['gx'=8,'gy'=4] {'gx'}, dimensions={0}, use_global_device_ids=true | all-gather | bytes 73728 | tf_op jit(solution)/shard_map/all_gather | solution.py:107
  70.8 9.2 %all-gather = f32[256,64]{1,0:T(8,128)S(1)} all-gather(f32[32,64]{1,0:T(8,128)S(1)} %add.268), channel_id=2, replica_groups=mesh['gx'=8,'gy'=4] {'gx'}, dimensions={0}, use_global_device_ids=true | all-gather | bytes 73728 | tf_op jit(solution)/shard_map/all_gather | solution.py:105
  86.1 2.7 %collective-permute-start.8 = (f32[32,64]{1,0:T(8,128)S(1)}, f32[32,64]{1,0:T(8,128)S(1)}, u32[]{:S(2)}, u32[]{:S(2)}) collective-permute-start(f32[32,64]{1,0:T(8,128)S(1)} %get-tuple-element.226), channel_id=1, source_target_pairs={{0,1},{1,0},{2,3},{3,2},{4,5},{5,4},{6,7},{7,6},{8,9},{9,8},{10,11... | collective-permute-start | bytes 24584 | tf_op jit(solution)/shard_map/ppermute | solution.py:11
  88.8 29.6 %all-reduce = (f32[32,64]{1,0:T(8,128)S(1)}, bf16[32,64]{1,0:T(8,128)(2,1)S(1)}) all-reduce(f32[32,64]{1,0:T(8,128)S(1)} %get-tuple-element.227, f32[32,64]{1,0:T(8,128)S(1)} %get-tuple-element.228), channel_id=1, replica_groups=mesh['gx'=8,'gy'=4] {'gy'}, use_global_device_ids=true, to_apply=%region_5.7 | all-reduce | flops 4096 | bytes 28672 | tf_op jit(solution)/shard_map/psum | solution.py:47
  120.3 3.1 %collective-permute-done.9 = f32[32,64]{1,0:T(8,128)S(1)} collective-permute-done((f32[32,64]{1,0:T(8,128)S(1)}, f32[32,64]{1,0:T(8,128)S(1)}, u32[]{:S(2)}, u32[]{:S(2)}) %collective-permute-start.9) | collective-permute-done | bytes 8224 | tf_op jit(solution)/shard_map/ppermute | solution.py:11
  125.7 122.9 %while.14 = (s32[]{:T(128)}, f32[8,64,256]{2,1,0:T(8,128)S(1)}, s32[8,24]{0,1:T(8,128)S(1)}, bf16[72,68,256]{2,1,0:T(8,128)(2,1)}, f32[8,24]{0,1:T(8,128)S(1)}, ...) while((s32[]{:T(128)}, f32[8,64,256]{2,1,0:T(8,128)S(1)}, ...), condition=%wide.region_1.2_spmd.clone, body=%wide.region_0.1_spmd.clone.sunk | while | flops 73833520 | bytes 2773931 | solution.py:95
  125.7 2.3 gather_fusion
  128.6 2.2 convolution_add_fusion.2
  130.9 2.3 gather_fusion
  133.7 2.2 convolution_add_fusion.2
  136.0 2.3 gather_fusion
  138.8 2.2 convolution_add_fusion.2
  141.1 2.3 gather_fusion
  143.9 2.2 convolution_add_fusion.2
  146.2 2.3 gather_fusion
  149.1 2.2 convolution_add_fusion.2
  151.4 2.3 gather_fusion
  156.5 2.3 gather_fusion
  161.6 2.3 gather_fusion
  166.7 2.3 gather_fusion
  171.8 2.3 gather_fusion
  177.0 2.3 gather_fusion
  179.8 2.2 convolution_add_fusion.2
  182.1 2.3 gather_fusion
  184.9 2.2 convolution_add_fusion.2
  187.2 2.3 gather_fusion
  190.1 2.2 convolution_add_fusion.2
  192.3 2.3 gather_fusion
  195.2 2.2 convolution_add_fusion.2
  197.5 2.3 gather_fusion
  202.6 2.3 gather_fusion
  207.7 2.3 gather_fusion
  212.8 2.3 gather_fusion
  218.0 2.3 gather_fusion
  223.1 2.3 gather_fusion
  225.9 2.2 convolution_add_fusion.2
  228.2 2.3 gather_fusion
  231.0 2.2 convolution_add_fusion.2
  233.3 2.3 gather_fusion
  236.2 2.2 convolution_add_fusion.2
  238.4 2.3 gather_fusion
  241.3 2.2 convolution_add_fusion.2
  243.6 2.3 gather_fusion
  (430 shorter events, 59.1 us)
Async XLA Ops:
  0.0 248.7 %copy-start = (bf16[1,1,4,32,8,256]{5,4,3,2,1,0:T(8,128)(2,1)S(1)}, bf16[1,1,4,32,8,256]{5,4,3,2,1,0:T(8,128)(2,1)}, u32[]{:S(2)}) copy-start(bf16[1,1,4,32,8,256]{5,4,3,2,1,0:T(8,128)(2,1)} %param.16) | copy-start | bytes 1572868
  0.0 44.4 %copy-start.3 = (s32[1,1,8,24]{3,2,1,0:T(8,128)S(1)}, s32[1,1,8,24]{3,2,1,0:T(8,128)}, u32[]{:S(2)}) copy-start(s32[1,1,8,24]{3,2,1,0:T(8,128)} %param.13) | copy-start | bytes 2308
  1.9 79.6 %collective-permute-start = (bf16[1,1,8,68,256]{4,2,1,0,3:T(8,128)(2,1)S(1)}, bf16[1,1,8,68,256]{4,2,1,0,3:T(8,128)(2,1)S(1)}, u32[]{:S(2)}, u32[]{:S(2)}) collective-permute-start(bf16[1,1,8,68,256]{4,2,1,0,3:T(8,128)(2,1)S(1)} %copy_dynamic-update-slice_fusion.1), channel_id=1, source_target_pairs={{0,4},{4,8},{8,12},{12,16},{16,20},{20,24},{24,28},{1,5},{5,9},{9,... | collective-permute-start | bytes 835592 | tf_op jit(solution)/shard_map/ppermute | solution.py:19
  4.3 77.3 %collective-permute-start.1 = (bf16[1,1,8,68,256]{4,2,1,0,3:T(8,128)(2,1)S(1)}, bf16[1,1,8,68,256]{4,2,1,0,3:T(8,128)(2,1)S(1)}, u32[]{:S(2)}, u32[]{:S(2)}) collective-permute-start(bf16[1,1,8,68,256]{4,2,1,0,3:T(8,128)(2,1)S(1)} %copy_dynamic-update-slice_fusion.1), channel_id=1, source_target_pairs={{4,0},{8,4},{12,8},{16,12},{20,16},{24,20},{28,24},{5,1},{9,5},{13... | collective-permute-start | bytes 835592 | tf_op jit(solution)/shard_map/ppermute | solution.py:22
  27.1 30.7 %collective-permute-start.6 = (f32[32,64]{1,0:T(8,128)S(1)}, f32[32,64]{1,0:T(8,128)S(1)}, u32[]{:S(2)}, u32[]{:S(2)}) collective-permute-start(f32[32,64]{1,0:T(8,128)S(1)} %get-tuple-element.207), channel_id=1, source_target_pairs={{0,4},{4,0},{8,12},{12,8},{16,20},{20,16},{24,28},{28,24},{1,5},{5... | collective-permute-start | bytes 24584 | tf_op jit(solution)/shard_map/ppermute | solution.py:11
  27.2 31.3 %collective-permute-start.4 = (f32[32,64]{1,0:T(8,128)S(1)}, f32[32,64]{1,0:T(8,128)S(1)}, u32[]{:S(2)}, u32[]{:S(2)}) collective-permute-start(f32[32,64]{1,0:T(8,128)S(1)} %get-tuple-element.232), channel_id=1, source_target_pairs={{0,1},{1,0},{2,3},{3,2},{4,5},{5,4},{6,7},{7,6},{8,9},{9,8},{10,11... | collective-permute-start | bytes 24584 | tf_op jit(solution)/shard_map/ppermute | solution.py:11
  57.9 3.8 %collective-permute-start.7 = (f32[32,64]{1,0:T(8,128)S(1)}, f32[32,64]{1,0:T(8,128)S(1)}, u32[]{:S(2)}, u32[]{:S(2)}) collective-permute-start(f32[32,64]{1,0:T(8,128)S(1)} %add.270), channel_id=1, source_target_pairs={{0,8},{4,12},{8,0},{12,4},{16,24},{20,28},{24,16},{28,20},{1,9},{5... | collective-permute-start | bytes 24584 | tf_op jit(solution)/shard_map/ppermute | solution.py:11
  58.5 12.3 %collective-permute-start.5 = (f32[32,64]{1,0:T(8,128)S(1)}, f32[32,64]{1,0:T(8,128)S(1)}, u32[]{:S(2)}, u32[]{:S(2)}) collective-permute-start(f32[32,64]{1,0:T(8,128)S(1)} %fusion.54), channel_id=1, source_target_pairs={{0,2},{1,3},{2,0},{3,1},{4,6},{5,7},{6,4},{7,5},{8,10},{9,11},{10,... | collective-permute-start | bytes 24584 | tf_op jit(solution)/shard_map/ppermute | solution.py:11
  61.7 19.2 %copy-start.4 = (f32[1,1,4,32,512]{4,3,2,1,0:T(8,128)S(1)}, f32[1,1,4,32,512]{4,3,2,1,0:T(8,128)}, u32[]{:S(2)}) copy-start(f32[1,1,4,32,512]{4,3,2,1,0:T(8,128)} %param.17) | copy-start | bytes 786436
  80.9 38.2 %copy-start.2 = (bf16[1,1,8,4,256]{4,3,2,1,0:T(4,128)(2,1)S(1)}, bf16[1,1,8,4,256]{4,3,2,1,0:T(4,128)(2,1)}, u32[]{:S(2)}) copy-start(bf16[1,1,8,4,256]{4,3,2,1,0:T(4,128)(2,1)} %param.12) | copy-start | bytes 49156
  82.6 40.8 %collective-permute-start.2 = (bf16[3,1,8,68,256]{4,2,3,1,0:T(8,128)(2,1)}, bf16[3,1,8,68,256]{4,2,3,1,0:T(8,128)(2,1)S(1)}, u32[]{:S(2)}, u32[]{:S(2)}) collective-permute-start(bf16[3,1,8,68,256]{4,2,3,1,0:T(8,128)(2,1)} %copy.46), channel_id=1, source_target_pairs={{0,1},{1,2},{2,3},{4,5},{5,6},{6,7},{8,9},{9,10},{10,11},{12,13},{... | collective-permute-start | bytes 2506760 | tf_op jit(solution)/shard_map/ppermute | solution.py:19
  84.8 38.7 %collective-permute-start.3 = (bf16[3,1,8,68,256]{4,2,3,1,0:T(8,128)(2,1)}, bf16[3,1,8,68,256]{4,2,3,1,0:T(8,128)(2,1)S(1)}, u32[]{:S(2)}, u32[]{:S(2)}) collective-permute-start(bf16[3,1,8,68,256]{4,2,3,1,0:T(8,128)(2,1)} %copy.46), channel_id=1, source_target_pairs={{1,0},{2,1},{3,2},{5,4},{6,5},{7,6},{9,8},{10,9},{11,10},{13,12},{... | collective-permute-start | bytes 2506760 | tf_op jit(solution)/shard_map/ppermute | solution.py:22
  86.1 32.4 %collective-permute-start.8 = (f32[32,64]{1,0:T(8,128)S(1)}, f32[32,64]{1,0:T(8,128)S(1)}, u32[]{:S(2)}, u32[]{:S(2)}) collective-permute-start(f32[32,64]{1,0:T(8,128)S(1)} %get-tuple-element.226), channel_id=1, source_target_pairs={{0,1},{1,0},{2,3},{3,2},{4,5},{5,4},{6,7},{7,6},{8,9},{9,8},{10,11... | collective-permute-start | bytes 24584 | tf_op jit(solution)/shard_map/ppermute | solution.py:11
  118.4 1.2 collective-permute-start.10
  118.5 4.8 %collective-permute-start.9 = (f32[32,64]{1,0:T(8,128)S(1)}, f32[32,64]{1,0:T(8,128)S(1)}, u32[]{:S(2)}, u32[]{:S(2)}) collective-permute-start(f32[32,64]{1,0:T(8,128)S(1)} %fusion.55), channel_id=1, source_target_pairs={{0,2},{1,3},{2,0},{3,1},{4,6},{5,7},{6,4},{7,5},{8,10},{9,11},{10,... | collective-permute-start | bytes 24584 | tf_op jit(solution)/shard_map/ppermute | solution.py:11
  119.7 3.7 %collective-permute-start.11 = (f32[32,64]{1,0:T(8,128)S(1)}, f32[32,64]{1,0:T(8,128)S(1)}, u32[]{:S(2)}, u32[]{:S(2)}) collective-permute-start(f32[32,64]{1,0:T(8,128)S(1)} %add.275), channel_id=1, source_target_pairs={{0,8},{4,12},{8,0},{12,4},{16,24},{20,28},{24,16},{28,20},{1,9},{5... | collective-permute-start | bytes 24584 | tf_op jit(solution)/shard_map/ppermute | solution.py:11
  123.7 2.1 copy-start.1
where the time goes:
time: 251 us; the launch traced here: 250 us
  blocking collectives  93 us (37%)
  local copies, waits for them, and re-layouts  67.1 us (27%)
  matrix products  56.5 us (23%)
  starting transfers between devices  12.5 us (5%)
  other arithmetic  12.2 us (5%)
  waiting for transfers between devices  5.95 us (2%)
    gather x24, local copies, waits for them, and re-layouts, add_slot(): chosen = jnp.take(block, index, axis=0)  55.6 us
    dot_general x24, matrix products, near_block(): jnp.einsum('lij,lrj->lri', kernel, source_vals, preferred_element_type=jn...  53.5 us
    psum x2, blocking collectives, column_level_sums(): second_sum, third_sum = lax.psum((second_term, third_term), 'gy')  49.7 us
    all_gather x1, blocking collectives, body(): column_table = lax.all_gather(projection[0][None], 'gy', axis=0, tiled=True)  13.1 us
    all_gather x1, blocking collectives, body(): lax.all_gather(second_sum[None], 'gx', axis=0, tiled=True)  12.6 us
    all_gather x1, blocking collectives, body(): lax.all_gather(first_sum[None], 'gx', axis=0, tiled=True)  9.15 us
    all_gather x1, blocking collectives, body(): lax.all_gather(third_sum[None], 'gx', axis=0, tiled=True)  8.41 us
    ppermute x8, waiting for transfers between devices, from_partner(): lax.ppermute(x, axis, [(i, i ^ 1 << stride) for i in range(lax.axis_size(...  5.94 us
  transfers between devices with their start and end apart: 12, of which 3 were waited for; matrix products, arithmetic and copies ran while one was open for 3% of the time, Pallas kernels for 0%

commit v1 on v0

--- a/solution.py
+++ b/solution.py
@@ -5,6 +5,28 @@
 from jax.sharding import PartitionSpec as P
 
 FOUR_PI = 4.0 * math.pi
+
+
+def in_order(blocks, dim):
+    blocks = jnp.moveaxis(blocks, 0, dim)
+    shape = blocks.shape
+    return blocks.reshape(*shape[:dim], shape[dim] * shape[dim + 1], *shape[dim + 2 :])
+
+
+def gather_around(x, axis, dim):
+    count = lax.axis_size(axis)
+    pairs = [(i, (i + 1) % count) for i in range(count)]
+    back = [(b, a) for a, b in pairs]
+    lower, upper = ([], [])
+    for step in range(count - 1):
+        if step % 2 == 0:
+            lower.append(lax.ppermute(lower[-1] if lower else x, axis, pairs))
+        else:
+            upper.append(lax.ppermute(upper[-1] if upper else x, axis, back))
+    pieces = jnp.stack([*lower[::-1], x, *upper])
+    shift = lax.axis_index(axis) - len(lower)
+    pieces = pieces[(jnp.arange(count) - shift) % count]
+    return in_order(pieces, dim)
 
 
 def from_partner(x, axis, stride):
@@ -102,7 +124,7 @@
     column_table = lax.all_gather(projection[0][None], "gy", axis=0, tiled=True)
     third_sum = coarse_total(column_three)
     table_one, table_two, table_three = (
-        lax.all_gather(first_sum[None], "gx", axis=0, tiled=True),
+        gather_around(first_sum[None], "gx", 0),
         lax.all_gather(second_sum[None], "gx", axis=0, tiled=True),
         lax.all_gather(third_sum[None], "gx", axis=0, tiled=True),
     )

time: 251 us -> 252 us (level)
  blocking collectives: 93 us -> 77.9 us
  starting transfers between devices: 12.5 us -> 22.6 us
  waiting for transfers between devices: 5.95 us -> 10.9 us
    all_gather x1 -> x0, blocking collectives: 9.15 us -> none  [body(): lax.all_gather(first_sum[None], 'gx', axis=0, tiled=True)]
    ppermute x0 -> x7, starting transfers between devices: none -> 5.77 us  [the longest x3 5.7 us: gather_around(): upper.append(lax.ppermute(upper[-1] if upper else x, axis, back))]
    ppermute x8, starting transfers between devices: 5.4 us -> 10.6 us  [from_partner(): lax.ppermute(x, axis, [(i, i ^ 1 << stride) for i in range(lax.axis_size(...]
    psum x2, blocking collectives: 49.7 us -> 46.2 us  [column_level_sums(): second_sum, third_sum = lax.psum((second_term, third_term), 'gy')]
    all_gather x1, blocking collectives: 12.6 us -> 9.24 us  [body(): lax.all_gather(second_sum[None], 'gx', axis=0, tiled=True)]
    ppermute x0 -> x7, waiting for transfers between devices: none -> 2.8 us  [the longest x3 2.79 us: gather_around(): upper.append(lax.ppermute(upper[-1] if upper else x, axis, back))]
  transfers between devices with their start and end apart: 12 -> 19, of which waited for: 3 -> 6; matrix products, arithmetic and copies ran while one was open for 3% -> 4% of each run, Pallas kernels for 0% -> 0%
where the time goes in v1:
time: 252 us; the launch traced here: 251 us
  blocking collectives  77.9 us (31%)
  local copies, waits for them, and re-layouts  67.7 us (27%)
  matrix products  56.5 us (22%)
  starting transfers between devices  22.6 us (9%)
  other arithmetic  12.9 us (5%)
  waiting for transfers between devices  10.9 us (4%)
    gather x24, local copies, waits for them, and re-layouts, add_slot(): chosen = jnp.take(block, index, axis=0)  55.6 us
    dot_general x24, matrix products, near_block(): jnp.einsum('lij,lrj->lri', kernel, source_vals, preferred_element_type=jn...  53.5 us
    psum x2, blocking collectives, column_level_sums(): second_sum, third_sum = lax.psum((second_term, third_term), 'gy')  46.2 us
    all_gather x1, blocking collectives, body(): column_table = lax.all_gather(projection[0][None], 'gy', axis=0, tiled=True)  13.2 us
    ppermute x8, starting transfers between devices, from_partner(): lax.ppermute(x, axis, [(i, i ^ 1 << stride) for i in range(lax.axis_size(...  10.6 us
    all_gather x1, blocking collectives, body(): lax.all_gather(second_sum[None], 'gx', axis=0, tiled=True)  9.24 us
    all_gather x1, blocking collectives, body(): lax.all_gather(third_sum[None], 'gx', axis=0, tiled=True)  9.23 us
    ppermute x8, waiting for transfers between devices, from_partner(): lax.ppermute(x, axis, [(i, i ^ 1 << stride) for i in range(lax.axis_size(...  8.14 us
  transfers between devices with their start and end apart: 19, of which 6 were waited for; matrix products, arithmetic and copies ran while one was open for 4% of the time, Pallas kernels for 0%

profile of v1, /device:TPU:0, one launch (start us, length us, event | category | flops | bytes accessed | tf_op | source)
XLA Modules:
  0.0 251.0 jit_solution(10748454129882271893)
XLA Ops:
  1.9 2.4 collective-permute-start
  7.0 2.5 collective-permute-start.4
  9.4 18.1 %all-reduce.1 = (f32[32,64]{1,0:T(8,128)S(1)}, f32[1,32,64]{2,1,0:T(8,128)S(1)}) all-reduce(f32[32,64]{1,0:T(8,128)S(1)} %get-tuple-element.230, f32[1,32,64]{2,1,0:T(8,128)S(1)} %get-tuple-element.231), channel_id=1, replica_groups=mesh['gx'=8,'gy'=4] {'gy'}, use_global_device_ids=true, to_apply=%region_3.5 | all-reduce | flops 4096 | bytes 32768 | tf_op jit(solution)/shard_map/psum | solution.py:69
  32.2 4.1 %collective-permute-done.5 = f32[32,64]{1,0:T(8,128)S(1)} collective-permute-done((f32[32,64]{1,0:T(8,128)S(1)}, f32[32,64]{1,0:T(8,128)S(1)}, u32[]{:S(2)}, u32[]{:S(2)}) %collective-permute-start.5) | collective-permute-done | bytes 8224 | tf_op jit(solution)/shard_map/ppermute | solution.py:33
  36.3 13.2 %all_gather.9 = f32[4,32,64]{2,1,0:T(8,128)S(1)} all-gather(f32[1,32,64]{2,1,0:T(8,128)S(1)} %get-tuple-element.229), channel_id=1, replica_groups=mesh['gx'=8,'gy'=4] {'gy'}, dimensions={0}, use_global_device_ids=true | all-gather | bytes 40960 | tf_op jit(solution)/shard_map/all_gather | solution.py:124
  50.6 4.1 %collective-permute-start.14 = (f32[32,64]{1,0:T(8,128)S(1)}, f32[32,64]{1,0:T(8,128)S(1)}, u32[]{:S(2)}, u32[]{:S(2)}) collective-permute-start(f32[32,64]{1,0:T(8,128)S(1)} %add.296), channel_id=1, source_target_pairs={{0,8},{4,12},{8,0},{12,4},{16,24},{20,28},{24,16},{28,20},{1,9},{5... | collective-permute-start | bytes 24584 | tf_op jit(solution)/shard_map/ppermute | solution.py:33
  54.7 9.2 %all_gather.10 = f32[8,32,64]{2,1,0:T(8,128)S(1)} all-gather(f32[1,32,64]{2,1,0:T(8,128)S(1)} %get-tuple-element.208), channel_id=1, replica_groups=mesh['gx'=8,'gy'=4] {'gx'}, dimensions={0}, use_global_device_ids=true | all-gather | bytes 73728 | tf_op jit(solution)/shard_map/all_gather | solution.py:128
  66.0 9.2 %all-gather = f32[256,64]{1,0:T(8,128)S(1)} all-gather(f32[32,64]{1,0:T(8,128)S(1)} %add.297), channel_id=2, replica_groups=mesh['gx'=8,'gy'=4] {'gx'}, dimensions={0}, use_global_device_ids=true | all-gather | bytes 73728 | tf_op jit(solution)/shard_map/all_gather | solution.py:129
  78.8 2.8 %collective-permute-start.12 = (f32[1,32,64]{2,1,0:T(8,128)S(1)}, f32[1,32,64]{2,1,0:T(8,128)S(1)}, u32[]{:S(2)}, u32[]{:S(2)}) collective-permute-start(f32[1,32,64]{2,1,0:T(8,128)S(1)} %collective-permute-done.11), channel_id=1, source_target_pairs={{4,0},{8,4},{12,8},{16,12},{20,16},{24,20},{28,24},{0,28},{5,1},{9... | collective-permute-start | bytes 24584 | tf_op jit(solution)/shard_map/ppermute | solution.py:25
  88.9 2.7 %collective-permute-start.15 = (f32[32,64]{1,0:T(8,128)S(1)}, f32[32,64]{1,0:T(8,128)S(1)}, u32[]{:S(2)}, u32[]{:S(2)}) collective-permute-start(f32[32,64]{1,0:T(8,128)S(1)} %get-tuple-element.226), channel_id=1, source_target_pairs={{0,1},{1,0},{2,3},{3,2},{4,5},{5,4},{6,7},{7,6},{8,9},{9,8},{10,11... | collective-permute-start | bytes 24584 | tf_op jit(solution)/shard_map/ppermute | solution.py:33
  91.6 28.1 %all-reduce = (f32[32,64]{1,0:T(8,128)S(1)}, bf16[32,64]{1,0:T(8,128)(2,1)S(1)}) all-reduce(f32[32,64]{1,0:T(8,128)S(1)} %get-tuple-element.227, f32[32,64]{1,0:T(8,128)S(1)} %get-tuple-element.228), channel_id=1, replica_groups=mesh['gx'=8,'gy'=4] {'gy'}, use_global_device_ids=true, to_apply=%region_5.7 | all-reduce | flops 4096 | bytes 28672 | tf_op jit(solution)/shard_map/psum | solution.py:69
  121.0 3.6 %collective-permute-done.16 = f32[32,64]{1,0:T(8,128)S(1)} collective-permute-done((f32[32,64]{1,0:T(8,128)S(1)}, f32[32,64]{1,0:T(8,128)S(1)}, u32[]{:S(2)}, u32[]{:S(2)}) %collective-permute-start.16) | collective-permute-done | bytes 8224 | tf_op jit(solution)/shard_map/ppermute | solution.py:33
  127.0 122.9 %while.14 = (s32[]{:T(128)}, f32[8,64,256]{2,1,0:T(8,128)S(1)}, s32[8,24]{0,1:T(8,128)S(1)}, bf16[72,68,256]{2,1,0:T(8,128)(2,1)}, f32[8,24]{0,1:T(8,128)S(1)}, ...) while((s32[]{:T(128)}, f32[8,64,256]{2,1,0:T(8,128)S(1)}, ...), condition=%wide.region_1.2_spmd.clone, body=%wide.region_0.1_spmd.clone.sunk | while | flops 73833520 | bytes 2773931 | solution.py:117
  127.0 2.3 gather_fusion
  129.9 2.2 convolution_add_fusion.2
  132.2 2.3 gather_fusion
  135.0 2.2 convolution_add_fusion.2
  137.3 2.3 gather_fusion
  142.4 2.3 gather_fusion
  147.5 2.3 gather_fusion
  150.4 2.2 convolution_add_fusion.2
  152.7 2.3 gather_fusion
  155.5 2.2 convolution_add_fusion.2
  157.8 2.3 gather_fusion
  160.6 2.2 convolution_add_fusion.2
  162.9 2.3 gather_fusion
  165.7 2.2 convolution_add_fusion.2
  168.0 2.3 gather_fusion
  173.2 2.3 gather_fusion
  178.3 2.3 gather_fusion
  183.4 2.3 gather_fusion
  188.5 2.3 gather_fusion
  193.6 2.3 gather_fusion
  198.8 2.3 gather_fusion
  201.6 2.2 convolution_add_fusion.2
  203.9 2.3 gather_fusion
  206.7 2.2 convolution_add_fusion.2
  209.0 2.3 gather_fusion
  211.9 2.2 convolution_add_fusion.2
  214.1 2.3 gather_fusion
  217.0 2.2 convolution_add_fusion.2
  219.3 2.3 gather_fusion
  224.4 2.3 gather_fusion
  229.5 2.3 gather_fusion
  234.6 2.3 gather_fusion
  239.8 2.3 gather_fusion
  244.9 2.3 gather_fusion
  247.7 2.2 convolution_add_fusion.2
  (452 shorter events, 68.5 us)
Async XLA Ops:
  0.0 250.0 %copy-start = (bf16[1,1,4,32,8,256]{5,4,3,2,1,0:T(8,128)(2,1)S(1)}, bf16[1,1,4,32,8,256]{5,4,3,2,1,0:T(8,128)(2,1)}, u32[]{:S(2)}) copy-start(bf16[1,1,4,32,8,256]{5,4,3,2,1,0:T(8,128)(2,1)} %param.16) | copy-start | bytes 1572868
  1.9 83.3 %collective-permute-start = (bf16[1,1,8,68,256]{4,2,1,0,3:T(8,128)(2,1)S(1)}, bf16[1,1,8,68,256]{4,2,1,0,3:T(8,128)(2,1)S(1)}, u32[]{:S(2)}, u32[]{:S(2)}) collective-permute-start(bf16[1,1,8,68,256]{4,2,1,0,3:T(8,128)(2,1)S(1)} %constant_dynamic-update-slice_fusion), channel_id=1, source_target_pairs={{0,4},{4,8},{8,12},{12,16},{16,20},{20,24},{24,28},{1,5},{5,9},{9,... | collective-permute-start | bytes 835592 | tf_op jit(solution)/shard_map/ppermute | solution.py:41
  4.3 80.9 %collective-permute-start.1 = (bf16[1,1,8,68,256]{4,2,1,0,3:T(8,128)(2,1)S(1)}, bf16[1,1,8,68,256]{4,2,1,0,3:T(8,128)(2,1)S(1)}, u32[]{:S(2)}, u32[]{:S(2)}) collective-permute-start(bf16[1,1,8,68,256]{4,2,1,0,3:T(8,128)(2,1)S(1)} %constant_dynamic-update-slice_fusion), channel_id=1, source_target_pairs={{4,0},{8,4},{12,8},{16,12},{20,16},{24,20},{28,24},{5,1},{9,5},{13... | collective-permute-start | bytes 835592 | tf_op jit(solution)/shard_map/ppermute | solution.py:44
  7.0 24.6 %collective-permute-start.4 = (f32[32,64]{1,0:T(8,128)S(1)}, f32[32,64]{1,0:T(8,128)S(1)}, u32[]{:S(2)}, u32[]{:S(2)}) collective-permute-start(f32[32,64]{1,0:T(8,128)S(1)} %get-tuple-element.232), channel_id=1, source_target_pairs={{0,1},{1,0},{2,3},{3,2},{4,5},{5,4},{6,7},{7,6},{8,9},{9,8},{10,11... | collective-permute-start | bytes 24584 | tf_op jit(solution)/shard_map/ppermute | solution.py:33
  27.6 23.0 %collective-permute-start.13 = (f32[32,64]{1,0:T(8,128)S(1)}, f32[32,64]{1,0:T(8,128)S(1)}, u32[]{:S(2)}, u32[]{:S(2)}) collective-permute-start(f32[32,64]{1,0:T(8,128)S(1)} %get-tuple-element.207), channel_id=1, source_target_pairs={{0,4},{4,0},{8,12},{12,8},{16,20},{20,16},{24,28},{28,24},{1,5},{5... | collective-permute-start | bytes 24584 | tf_op jit(solution)/shard_map/ppermute | solution.py:33
  31.6 4.7 %collective-permute-start.5 = (f32[32,64]{1,0:T(8,128)S(1)}, f32[32,64]{1,0:T(8,128)S(1)}, u32[]{:S(2)}, u32[]{:S(2)}) collective-permute-start(f32[32,64]{1,0:T(8,128)S(1)} %fusion.56), channel_id=1, source_target_pairs={{0,2},{1,3},{2,0},{3,1},{4,6},{5,7},{6,4},{7,5},{8,10},{9,11},{10,... | collective-permute-start | bytes 24584 | tf_op jit(solution)/shard_map/ppermute | solution.py:33
  36.3 18.3 %collective-permute-start.6 = (f32[1,32,64]{2,1,0:T(8,128)S(1)}, f32[1,32,64]{2,1,0:T(8,128)S(1)}, u32[]{:S(2)}, u32[]{:S(2)}) collective-permute-start(f32[1,32,64]{2,1,0:T(8,128)S(1)} %add_bitcast_fusion), channel_id=1, source_target_pairs={{0,4},{4,8},{8,12},{12,16},{16,20},{20,24},{24,28},{28,0},{1,5},{5... | collective-permute-start | bytes 24584 | tf_op jit(solution)/shard_map/ppermute | solution.py:23
  50.6 15.4 %collective-permute-start.14 = (f32[32,64]{1,0:T(8,128)S(1)}, f32[32,64]{1,0:T(8,128)S(1)}, u32[]{:S(2)}, u32[]{:S(2)}) collective-permute-start(f32[32,64]{1,0:T(8,128)S(1)} %add.296), channel_id=1, source_target_pairs={{0,8},{4,12},{8,0},{12,4},{16,24},{20,28},{24,16},{28,20},{1,9},{5... | collective-permute-start | bytes 24584 | tf_op jit(solution)/shard_map/ppermute | solution.py:33
  54.7 11.3 %collective-permute-start.7 = (f32[1,32,64]{2,1,0:T(8,128)S(1)}, f32[1,32,64]{2,1,0:T(8,128)S(1)}, u32[]{:S(2)}, u32[]{:S(2)}) collective-permute-start(f32[1,32,64]{2,1,0:T(8,128)S(1)} %collective-permute-done.6), channel_id=1, source_target_pairs={{0,4},{4,8},{8,12},{12,16},{16,20},{20,24},{24,28},{28,0},{1,5},{5... | collective-permute-start | bytes 24584 | tf_op jit(solution)/shard_map/ppermute | solution.py:23
  64.5 11.5 %collective-permute-start.10 = (f32[1,32,64]{2,1,0:T(8,128)S(1)}, f32[1,32,64]{2,1,0:T(8,128)S(1)}, u32[]{:S(2)}, u32[]{:S(2)}) collective-permute-start(f32[1,32,64]{2,1,0:T(8,128)S(1)} %add_bitcast_fusion), channel_id=1, source_target_pairs={{4,0},{8,4},{12,8},{16,12},{20,16},{24,20},{28,24},{0,28},{5,1},{9... | collective-permute-start | bytes 24584 | tf_op jit(solution)/shard_map/ppermute | solution.py:25
  65.9 11.5 %collective-permute-start.8 = (f32[1,32,64]{2,1,0:T(8,128)S(1)}, f32[1,32,64]{2,1,0:T(8,128)S(1)}, u32[]{:S(2)}, u32[]{:S(2)}) collective-permute-start(f32[1,32,64]{2,1,0:T(8,128)S(1)} %collective-permute-done.7), channel_id=1, source_target_pairs={{0,4},{4,8},{8,12},{12,16},{16,20},{20,24},{24,28},{28,0},{1,5},{5... | collective-permute-start | bytes 24584 | tf_op jit(solution)/shard_map/ppermute | solution.py:23
  75.2 9.3 %copy-start.3 = (f32[1,1,4,32,512]{4,3,2,1,0:T(8,128)S(1)}, f32[1,1,4,32,512]{4,3,2,1,0:T(8,128)}, u32[]{:S(2)}) copy-start(f32[1,1,4,32,512]{4,3,2,1,0:T(8,128)} %param.17) | copy-start | bytes 786436
  75.9 2.9 %collective-permute-start.11 = (f32[1,32,64]{2,1,0:T(8,128)S(1)}, f32[1,32,64]{2,1,0:T(8,128)S(1)}, u32[]{:S(2)}, u32[]{:S(2)}) collective-permute-start(f32[1,32,64]{2,1,0:T(8,128)S(1)} %collective-permute-done.10), channel_id=1, source_target_pairs={{4,0},{8,4},{12,8},{16,12},{20,16},{24,20},{28,24},{0,28},{5,1},{9... | collective-permute-start | bytes 24584 | tf_op jit(solution)/shard_map/ppermute | solution.py:25
  77.4 4.2 %collective-permute-start.9 = (f32[1,32,64]{2,1,0:T(8,128)S(1)}, f32[1,32,64]{2,1,0:T(8,128)S(1)}, u32[]{:S(2)}, u32[]{:S(2)}) collective-permute-start(f32[1,32,64]{2,1,0:T(8,128)S(1)} %collective-permute-done.8), channel_id=1, source_target_pairs={{0,4},{4,8},{8,12},{12,16},{16,20},{20,24},{24,28},{28,0},{1,5},{5... | collective-permute-start | bytes 24584 | tf_op jit(solution)/shard_map/ppermute | solution.py:23
  78.8 4.2 %collective-permute-start.12 = (f32[1,32,64]{2,1,0:T(8,128)S(1)}, f32[1,32,64]{2,1,0:T(8,128)S(1)}, u32[]{:S(2)}, u32[]{:S(2)}) collective-permute-start(f32[1,32,64]{2,1,0:T(8,128)S(1)} %collective-permute-done.11), channel_id=1, source_target_pairs={{4,0},{8,4},{12,8},{16,12},{20,16},{24,20},{28,24},{0,28},{5,1},{9... | collective-permute-start | bytes 24584 | tf_op jit(solution)/shard_map/ppermute | solution.py:25
  84.6 35.9 %copy-start.2 = (bf16[1,1,8,4,256]{4,3,2,1,0:T(4,128)(2,1)S(1)}, bf16[1,1,8,4,256]{4,3,2,1,0:T(4,128)(2,1)}, u32[]{:S(2)}) copy-start(bf16[1,1,8,4,256]{4,3,2,1,0:T(4,128)(2,1)} %param.12) | copy-start | bytes 49156
  86.3 38.5 %collective-permute-start.2 = (bf16[3,1,8,68,256]{4,2,3,1,0:T(8,128)(2,1)}, bf16[3,1,8,68,256]{4,2,3,1,0:T(8,128)(2,1)S(1)}, u32[]{:S(2)}, u32[]{:S(2)}) collective-permute-start(bf16[3,1,8,68,256]{4,2,3,1,0:T(8,128)(2,1)} %copy.46), channel_id=1, source_target_pairs={{0,1},{1,2},{2,3},{4,5},{5,6},{6,7},{8,9},{9,10},{10,11},{12,13},{... | collective-permute-start | bytes 2506760 | tf_op jit(solution)/shard_map/ppermute | solution.py:41
  87.6 37.1 %collective-permute-start.3 = (bf16[3,1,8,68,256]{4,2,3,1,0:T(8,128)(2,1)}, bf16[3,1,8,68,256]{4,2,3,1,0:T(8,128)(2,1)S(1)}, u32[]{:S(2)}, u32[]{:S(2)}) collective-permute-start(bf16[3,1,8,68,256]{4,2,3,1,0:T(8,128)(2,1)} %copy.46), channel_id=1, source_target_pairs={{1,0},{2,1},{3,2},{5,4},{6,5},{7,6},{9,8},{10,9},{11,10},{13,12},{... | collective-permute-start | bytes 2506760 | tf_op jit(solution)/shard_map/ppermute | solution.py:44
  88.9 30.9 %collective-permute-start.15 = (f32[32,64]{1,0:T(8,128)S(1)}, f32[32,64]{1,0:T(8,128)S(1)}, u32[]{:S(2)}, u32[]{:S(2)}) collective-permute-start(f32[32,64]{1,0:T(8,128)S(1)} %get-tuple-element.226), channel_id=1, source_target_pairs={{0,1},{1,0},{2,3},{3,2},{4,5},{5,4},{6,7},{7,6},{8,9},{9,8},{10,11... | collective-permute-start | bytes 24584 | tf_op jit(solution)/shard_map/ppermute | solution.py:33
  119.7 1.2 collective-permute-start.17
  119.8 4.7 %collective-permute-start.16 = (f32[32,64]{1,0:T(8,128)S(1)}, f32[32,64]{1,0:T(8,128)S(1)}, u32[]{:S(2)}, u32[]{:S(2)}) collective-permute-start(f32[32,64]{1,0:T(8,128)S(1)} %fusion.57), channel_id=1, source_target_pairs={{0,2},{1,3},{2,0},{3,1},{4,6},{5,7},{6,4},{7,5},{8,10},{9,11},{10,... | collective-permute-start | bytes 24584 | tf_op jit(solution)/shard_map/ppermute | solution.py:33
  121.0 3.7 %collective-permute-start.18 = (f32[32,64]{1,0:T(8,128)S(1)}, f32[32,64]{1,0:T(8,128)S(1)}, u32[]{:S(2)}, u32[]{:S(2)}) collective-permute-start(f32[32,64]{1,0:T(8,128)S(1)} %add.301), channel_id=1, source_target_pairs={{0,8},{4,12},{8,0},{12,4},{16,24},{20,28},{24,16},{28,20},{1,9},{5... | collective-permute-start | bytes 24584 | tf_op jit(solution)/shard_map/ppermute | solution.py:33
  125.0 2.0 copy-start.1
